TPU v7x, 1024 devices: a whole 4x4x32 slice. The times are simulated.
1024 devices in a mesh: energy: 128 (over z, x), slab: 4 (over y_hi, core), rep: 2 (over y_lo).
Axes of the slice: x: 4, y: 4 (y_hi: 2, y_lo: 2; y = y_hi * 2 + y_lo), z: 32, core: 2. Of those that a mesh axis runs over, the one named last changes fastest.
Arguments:
- green_blocks: bfloat16 [128, 4, 512, 512], P('energy', 'slab', 'rep'), may hold values from -1 to 1
- occupation: float32 [128], P('energy'), may hold values from 0.1 to 1
- offsets: int32 [2], replicated, may hold values from 1 to 4, as said below
- coulomb: float32 [4, 512, 512], P('slab', 'rep'), may hold values from -0.9 to 0.9
- hamiltonian: float32 [4, 512, 512], P('slab', 'rep'), may hold values from -0.25 to 0.25
- onsite_level: float32 [128], P('energy'), may hold values from 2 to 3
- green_steps: int32 [128], P('energy'), may hold values from 1 to 2, as said below
- screen_steps: int32 [2], replicated, may hold values from 0 to 2, as said below
Outputs:
- green_next: float32 [128, 4, 512, 512], P('energy', 'slab', 'rep')
- screened: bfloat16 [2, 4, 512, 512], P(None, 'slab', 'rep')
Inputs may be any that keep to these rules, and one draw needn't show every extreme that they name: `offsets`: some frequency has offset 4; every other frequency has a smaller one. `green_steps`: some energy takes 2 turns. `screen_steps`: some frequency takes 2 turns; every other frequency takes fewer.
All inputs are finite; a program needn't handle non-finite values.
Results may differ from a plain program's by a relative error of at most 0.0004.
Values may be sent and summed in bfloat16 or wider, within the bound.
A program may use at most 32 MiB of HBM per device.

v0:
```python
import jax
import jax.numpy as jnp
from jax import lax
from jax.sharding import PartitionSpec as P

SHIFTS = 4
FREQS = 2
NG = 2
NW = 2


precise = lax.Precision.HIGHEST


def from_behind(block, axis, distance):
    devices = range(lax.axis_size(axis))
    route = [(i - distance, i) for i in devices if i - distance in devices]
    return lax.ppermute(block, axis, route)


def broadcast(block, axis, owner):
    block = jnp.where(lax.axis_index(axis) == owner, block, jnp.zeros_like(block))
    return lax.psum(block, axis)


def with_halo(value, sides, width):
    for axis, dim in sides:
        peers, length = (lax.axis_size(axis), value.shape[dim])
        up = [(i, (i + 1) % peers) for i in range(peers - 1)]
        down = [(j, i) for i, j in up]
        last = lax.slice_in_dim(value, length - width, length, axis=dim)
        first = lax.slice_in_dim(value, 0, width, axis=dim)
        before = lax.ppermute(last, axis, up)
        after = lax.ppermute(first, axis, down)
        value = jnp.concatenate([before, value, after], axis=dim)
    return value


def row_product(first_factor, second_factor):
    return jnp.einsum("esij,esjk->esik", first_factor, second_factor, precision=precise)


def full_rows(block_rows):
    return lax.all_gather(block_rows, "rep", axis=2, tiled=True)


def newton_rows(operator, initial, known_full, counts, turn_total):
    iterate = initial
    for turn_index in range(turn_total):
        if turn_index == 0 and known_full is not None:
            iterate_full = known_full
        else:
            iterate_full = full_rows(iterate)
        applied = row_product(operator, iterate_full)
        applied_full = lax.all_gather(applied, "rep", axis=2, tiled=True)
        composed = row_product(iterate, applied_full)
        iterate = jnp.where(
            (turn_index < counts)[:, None, None, None], 2.0 * iterate - composed, iterate
        )
    return iterate


def body(
    green_blocks, occupation, offsets, coulomb, hamiltonian, onsite_level, green_steps, screen_steps
):
    local_count, _, half_rows, full_width = green_blocks.shape
    energies = local_count * lax.axis_size("energy")
    entry_scale = full_width ** (-0.5)
    shift_count = -(-SHIFTS // local_count)
    pieces = []
    received = green_blocks
    for distance in range(1, shift_count + 1):
        received = from_behind(received, "energy", 1)
        pieces.insert(0, received)
    extended = jnp.concatenate(pieces + [green_blocks], axis=0)
    anchor = shift_count * local_count
    lowered = jnp.stack(
        [
            lax.dynamic_slice_in_dim(extended, anchor - offsets[index], local_count, 0)
            for index in range(FREQS)
        ]
    )
    lowered_wide = lowered.astype(jnp.float32)
    weighted = occupation[:, None, None, None] * green_blocks.astype(jnp.float32)
    partial_value = jnp.sum(weighted[None] * lowered_wide, axis=1) * energies ** (-0.5)
    polarization = lax.psum(partial_value, "energy")
    rep_start = lax.axis_index("rep") * half_rows
    col_index = lax.broadcasted_iota(jnp.int32, (half_rows, full_width), 1)
    row_index = lax.broadcasted_iota(jnp.int32, (half_rows, full_width), 0) + rep_start
    identity_rows = (col_index == row_index).astype(jnp.float32)
    identity_full = jnp.eye(full_width, dtype=jnp.float32)[None, None]
    owner_index = lax.axis_index("energy") % FREQS
    polar_own = lax.dynamic_index_in_dim(polarization, owner_index, 0, keepdims=True)
    screen_operator = identity_rows + entry_scale * coulomb[None] * polar_own
    count_own = lax.dynamic_index_in_dim(screen_steps, owner_index, 0, keepdims=True)
    screen_start = jnp.broadcast_to(identity_rows, screen_operator.shape)
    inverse = newton_rows(screen_operator, screen_start, identity_full, count_own, NW)
    inverse_full = full_rows(inverse)
    screened_own = row_product(coulomb[None], inverse_full).astype(jnp.bfloat16)
    screened = jnp.stack([broadcast(screened_own, "energy", index)[0] for index in range(FREQS)])
    self_energy = (
        jnp.sum(lowered_wide * screened.astype(jnp.float32)[:, None], axis=0) * entry_scale
    )
    neighbours = with_halo(green_blocks, (("slab", 1),), 1)
    contact = (neighbours[:, 0:1].astype(jnp.float32) + neighbours[:, 2:3].astype(jnp.float32)) * (
        0.5 * entry_scale
    )
    dyson_rows = (
        onsite_level[:, None, None, None] * identity_rows
        + hamiltonian[None]
        - self_energy
        - contact
    )
    diagonal = jnp.sum(dyson_rows * identity_rows, axis=-1)
    initial = identity_rows * (1.0 / diagonal)[..., None]
    green_next = newton_rows(dyson_rows, initial, None, green_steps, NG)
    return (green_next, screened)


def solution(mesh):
    return jax.shard_map(
        body,
        mesh=mesh,
        in_specs=(
            P("energy", "slab", "rep", None),
            P("energy"),
            P(),
            P("slab", "rep", None),
            P("slab", "rep", None),
            P("energy"),
            P("energy"),
            P(),
        ),
        out_specs=(P("energy", "slab", "rep", None), P(None, "slab", "rep", None)),
        check_vma=False,
    )
```

profile of v0, /device:TPU:6, one launch (start us, length us, event | category | flops | bytes accessed | tf_op | source)
XLA Modules:
  0.0 1438.1 jit_solution(3436716739450063870)
XLA Ops:
  7.2 0.0 all-reduce.4.cloned.1.call-start
  7.2 1.1 copy.17
  8.3 3.7 collective-permute-start
  12.0 6.2 collective-permute-done
  18.2 5.8 collective-permute-start.1
  24.1 4.7 collective-permute-done.1
  28.8 6.5 collective-permute-start.2
  35.3 6.8 collective-permute-done.2
  42.1 3.5 collective-permute-start.3
  45.6 1.3 fusion.30
  50.2 1.0 multiply_bitcast_fusion
  51.2 0.2 copy.20
  51.6 0.0 copy-start.2
  51.6 1.1 multiply_multiply_fusion
  52.7 0.0 all-reduce.4.cloned.1.call-update
  52.7 0.0 all-gather.18.cloned.1.call-start
  52.8 0.2 copy.19
  53.0 0.0 copy-start.7
  53.0 516.4 %all-reduce.4.cloned.1.call-done = f32[2,1,256,512]{2,3,1,0:T(8,128)} async-done(((f32[2,1,256,512]{2,3,1,0:T(8,128)}), f32[2,1,256,512]{2,3,1,0:T(8,128)}) %all-reduce.4.cloned.1.call-update) | async-done | bytes 1048592 | tf_op jit(solution)/shard_map/psum | solution.py:86
  569.5 2.5 fusion.7
  572.0 0.0 all-gather.18.cloned.1.call-update
  572.0 0.0 all-gather.20.cloned.1.call-start
  572.1 0.7 dynamic_slice.16
  573.5 32.3 %all-gather.18.cloned.1.call-done = f32[512,512]{1,0:T(8,128)} async-done(((f32[256,512]{1,0:T(8,128)}), f32[512,512]{1,0:T(8,128)}) %all-gather.18.cloned.1.call-update) | async-done | bytes 1048592 | tf_op jit(solution)/shard_map/all_gather | solution.py:55
  605.8 2.8 fusion.4
  608.5 0.0 all-gather.20.cloned.1.call-update
  608.6 0.0 all-gather.22.cloned.1.call-start
  608.6 43.7 %all-gather.20.cloned.1.call-done = f32[512,512]{1,0:T(8,128)} async-done(((f32[256,512]{1,0:T(8,128)}), f32[512,512]{1,0:T(8,128)}) %all-gather.20.cloned.1.call-update) | async-done | bytes 1048592 | tf_op jit(solution)/shard_map/all_gather | solution.py:44
  652.3 3.1 fusion.15
  655.5 0.0 all-gather.22.cloned.1.call-update
  655.5 0.0 all-gather.24.cloned.1.call-start
  656.2 42.5 %all-gather.22.cloned.1.call-done = f32[512,512]{1,0:T(8,128)} async-done(((f32[256,512]{1,0:T(8,128)}), f32[512,512]{1,0:T(8,128)}) %all-gather.22.cloned.1.call-update) | async-done | bytes 1048592 | tf_op jit(solution)/shard_map/all_gather | solution.py:55
  698.7 3.1 fusion.1
  701.8 0.0 all-gather.24.cloned.1.call-update
  701.8 0.0 all-reduce.6.cloned.1.call-start
  701.9 43.2 %all-gather.24.cloned.1.call-done = f32[512,512]{1,0:T(8,128)} async-done(((f32[256,512]{1,0:T(8,128)}), f32[512,512]{1,0:T(8,128)}) %all-gather.24.cloned.1.call-update) | async-done | bytes 1048592 | tf_op jit(solution)/shard_map/all_gather | solution.py:44
  745.1 3.8 select_bitcast_fusion.1
  748.9 0.0 all-reduce.6.cloned.1.call-update
  749.0 0.0 all-gather.16.cloned.1.call-start
  749.0 1.8 collective-permute-start.4
  750.8 1.3 collective-permute-start.5
  752.1 0.2 copy.16
  752.9 499.9 %all-reduce.6.cloned.1.call-done = (bf16[1,1,256,512]{2,3,1,0:T(8,128)(2,1)}, bf16[1,1,256,512]{2,3,1,0:T(8,128)(2,1)}) async-done(((bf16[1,1,256,512]{2,3,1,0:T(8,128)(2,1)}, bf16[1,1,256,512]{2,3,1,0:T(8,128)(2,1)}), (bf16[1,1,256,512]{2,3,1,0:T(8,128)(2,1)}, bf16[1,1,256,512]{2,3,1,0:T(8,128)(2,1)})) %all-reduce.6.cloned.1.call-update) | async-done | bytes 524304 | tf_op jit(solution)/shard_map/psum | solution.py:23
  1252.8 1.2 multiply_reduce_fusion
  1254.1 0.2 select_reduce_fusion
  1254.3 0.8 fusion.19
  1255.1 0.0 all-gather.16.cloned.1.call-update
  1255.2 0.0 all-gather.26.cloned.1.call-start
  1255.2 33.7 %all-gather.16.cloned.1.call-done = f32[1,1,512,512]{2,3,1,0:T(8,128)} async-done(((f32[1,1,256,512]{2,3,1,0:T(8,128)}), f32[1,1,512,512]{2,3,1,0:T(8,128)}) %all-gather.16.cloned.1.call-update) | async-done | bytes 1048592 | tf_op jit(solution)/shard_map/all_gather | solution.py:44
  1288.9 3.9 fusion.5
  1292.8 0.0 all-gather.26.cloned.1.call-update
  1292.8 0.0 all-gather.28.cloned.1.call-start
  1293.5 1.1 compare_select_fusion
  1294.6 41.3 %all-gather.26.cloned.1.call-done = f32[512,512]{1,0:T(8,128)} async-done(((f32[256,512]{1,0:T(8,128)}), f32[512,512]{1,0:T(8,128)}) %all-gather.26.cloned.1.call-update) | async-done | bytes 1048592 | tf_op jit(solution)/shard_map/all_gather | solution.py:55
  1335.9 3.1 fusion.2
  1338.9 0.0 all-gather.28.cloned.1.call-update
  1339.0 0.2 all-gather.30.cloned.1.call-start
  1339.2 42.8 %all-gather.28.cloned.1.call-done = f32[512,512]{1,0:T(8,128)} async-done(((f32[256,512]{1,0:T(8,128)}), f32[512,512]{1,0:T(8,128)}) %all-gather.28.cloned.1.call-update) | async-done | bytes 1048592 | tf_op jit(solution)/shard_map/all_gather | solution.py:44
  1382.0 3.1 fusion.10
  1385.1 0.0 all-gather.30.cloned.1.call-update
  1385.2 0.1 pad_maximum_fusion
  1385.2 1.0 copy.23
  1386.3 42.0 %all-gather.30.cloned.1.call-done = f32[512,512]{1,0:T(8,128)} async-done(((f32[256,512]{1,0:T(8,128)}), f32[512,512]{1,0:T(8,128)}) %all-gather.30.cloned.1.call-update) | async-done | bytes 1048592 | tf_op jit(solution)/shard_map/all_gather | solution.py:55
  1428.2 3.1 fusion.3
  (25 shorter events, 0.2 us)
Async XLA Ops:
  7.2 562.3 %all-reduce.4.cloned.1.call-start = ((), (), s32[]{:S(2)}) async-start(), calls=%async_computation | async-start | bytes 2097152 | tf_op jit(solution)/shard_map/psum | solution.py:86
  8.3 9.9 collective-permute-start
  18.2 10.5 collective-permute-start.1
  28.8 13.3 collective-permute-start.2
  42.1 9.3 collective-permute-start.3
  51.6 1.2 copy-start.2
  52.7 553.0 %all-gather.18.cloned.1.call-start = ((), (), s32[]{:S(2)}) async-start(), calls=%async_computation.2 | async-start | bytes 1572864 | tf_op jit(solution)/shard_map/all_gather | solution.py:55
  53.0 519.1 %copy-start.7 = (s32[2]{0:T(128)S(1)}, s32[2]{0:T(128)}, u32[]{:S(2)}) copy-start(s32[2]{0:T(128)} %param.15) | copy-start | bytes 28
  572.0 80.3 %copy-start.3 = (f32[2,1,256,512]{2,3,1,0:T(8,128)S(1)}, f32[2,1,256,512]{2,3,1,0:T(8,128)}, u32[]{:S(2)}) copy-start(f32[2,1,256,512]{2,3,1,0:T(8,128)} %all-reduce.4.cloned.1.call-done) | copy-start | bytes 3145732
  572.0 80.3 %all-gather.20.cloned.1.call-start = ((), (), s32[]{:S(2)}) async-start(), calls=%async_computation.3 | async-start | bytes 1572864 | tf_op jit(solution)/shard_map/all_gather | solution.py:44
  608.6 90.2 %copy-start = (f32[256,512]{1,0:T(8,128)S(1)}, f32[256,512]{1,0:T(8,128)}, u32[]{:S(2)}) copy-start(f32[256,512]{1,0:T(8,128)} %fusion.4) | copy-start | bytes 1572868
  608.6 90.2 %all-gather.22.cloned.1.call-start = ((), (), s32[]{:S(2)}) async-start(), calls=%async_computation.4 | async-start | bytes 1572864 | tf_op jit(solution)/shard_map/all_gather | solution.py:55
  655.5 89.6 %all-gather.24.cloned.1.call-start = ((), (), s32[]{:S(2)}) async-start(), calls=%async_computation.5 | async-start | bytes 1572864 | tf_op jit(solution)/shard_map/all_gather | solution.py:44
  701.8 551.0 %all-reduce.6.cloned.1.call-start = ((), (), s32[]{:S(2)}) async-start(), calls=%async_computation.9 | async-start | bytes 1048576 | tf_op jit(solution)/shard_map/psum | solution.py:23
  701.9 50.2 %copy-start.6 = (f32[1,256,512]{2,1,0:T(8,128)S(1)}, f32[1,256,512]{2,1,0:T(8,128)}, u32[]{:S(2)}) copy-start(f32[1,256,512]{2,1,0:T(8,128)} %param.12) | copy-start | bytes 1572868
  749.0 539.9 %all-gather.16.cloned.1.call-start = ((), (), s32[]{:S(2)}) async-start(), calls=%async_computation.1 | async-start | bytes 1572864 | tf_op jit(solution)/shard_map/all_gather | solution.py:44
  749.0 505.0 %collective-permute-start.4 = (bf16[1,1,256,512]{2,3,1,0:T(8,128)(2,1)S(1)}, bf16[1,1,256,512]{2,3,1,0:T(8,128)(2,1)S(1)}, u32[]{:S(2)}, u32[]{:S(2)}) collective-permute-start(bf16[1,1,256,512]{2,3,1,0:T(8,128)(2,1)S(1)} %copy.17), channel_id=1, source_target_pairs={{0,2},{2,4},{4,6},{1,3},{3,5},{5,7},{8,10},{10,12},{12,14},{9,11},... | collective-permute-start | bytes 786440 | tf_op jit(solution)/shard_map/ppermute | solution.py:33
  750.8 503.3 %collective-permute-start.5 = (bf16[1,1,256,512]{2,3,1,0:T(8,128)(2,1)S(1)}, bf16[1,1,256,512]{2,3,1,0:T(8,128)(2,1)S(1)}, u32[]{:S(2)}, u32[]{:S(2)}) collective-permute-start(bf16[1,1,256,512]{2,3,1,0:T(8,128)(2,1)S(1)} %copy.17), channel_id=1, source_target_pairs={{2,0},{4,2},{6,4},{3,1},{5,3},{7,5},{10,8},{12,10},{14,12},{11,9},... | collective-permute-start | bytes 786440 | tf_op jit(solution)/shard_map/ppermute | solution.py:34
  1255.2 80.7 %all-gather.26.cloned.1.call-start = ((), (), s32[]{:S(2)}) async-start(), calls=%async_computation.6 | async-start | bytes 1572864 | tf_op jit(solution)/shard_map/all_gather | solution.py:55
  1292.8 89.3 %all-gather.28.cloned.1.call-start = ((), (), s32[]{:S(2)}) async-start(), calls=%async_computation.7 | async-start | bytes 1572864 | tf_op jit(solution)/shard_map/all_gather | solution.py:44
  1339.0 46.2 %copy-start.4 = (bf16[1,1,256,512]{2,3,1,0:T(8,128)(2,1)S(1)}, bf16[1,1,256,512]{2,3,1,0:T(8,128)(2,1)}, u32[]{:S(2)}) copy-start(bf16[1,1,256,512]{2,3,1,0:T(8,128)(2,1)} %get-tuple-element.8) | copy-start | bytes 786436
  1339.0 46.2 %copy-start.5 = (bf16[1,1,256,512]{2,3,1,0:T(8,128)(2,1)S(1)}, bf16[1,1,256,512]{2,3,1,0:T(8,128)(2,1)}, u32[]{:S(2)}) copy-start(bf16[1,1,256,512]{2,3,1,0:T(8,128)(2,1)} %get-tuple-element.9) | copy-start | bytes 786436
  1339.0 89.2 %all-gather.30.cloned.1.call-start = ((), (), s32[]{:S(2)}) async-start(), calls=%async_computation.8 | async-start | bytes 1572864 | tf_op jit(solution)/shard_map/all_gather | solution.py:55
  1385.1 43.1 %copy-start.1 = (f32[256,512]{1,0:T(8,128)S(1)}, f32[256,512]{1,0:T(8,128)}, u32[]{:S(2)}) copy-start(f32[256,512]{1,0:T(8,128)} %fusion.2) | copy-start | bytes 1572868
Sparse Core Ops, SparseCore 0:
  52.9 516.5 all-reduce.3
  573.1 32.6 all-gather.17
  609.4 42.8 all-gather.19
  655.8 42.8 all-gather.21
  702.2 42.8 all-gather.23
  749.4 503.3 all-reduce.5
  1256.1 32.7 all-gather.15
  1292.9 42.8 all-gather.25
  1339.1 42.8 all-gather.27
  1385.3 42.8 all-gather.29
where the time goes:
time: 1440 us
  waiting for transfers between devices  1360 us (94%)
  matrix products  28.5 us (2%)
  starting transfers between devices  23.2 us (2%)
  between operations  20.4 us (1%)
    psum x1, waiting for transfers between devices, body(): polarization = lax.psum(partial_value, 'energy')  516 us
    psum x1, waiting for transfers between devices, broadcast(): return lax.psum(block, axis)  500 us
    all_gather x4, waiting for transfers between devices, full_rows(): return lax.all_gather(block_rows, 'rep', axis=2, tiled=True)  163 us
    all_gather x4, waiting for transfers between devices, newton_rows(): applied_full = lax.all_gather(applied, 'rep', axis=2, tiled=True)  158 us
  transfers between devices with their start and end apart: 16, of which 13 were waited for; matrix products, arithmetic and copies ran while one was open for 0% of the time, Pallas kernels for 0%

commit v1 on v0

v1 whole, which is shorter than its diff:
```python
import functools
import jax
import jax.numpy as jnp
from jax import lax
from jax.sharding import PartitionSpec as P
import jax.experimental.pallas as pl
import jax.experimental.pallas.tpu as pltpu

MESH = pl.DeviceIdType.MESH
B = 512
H = 256
XN = 4
ZN = 32
E = XN * ZN
F32 = jnp.float32
BF16 = jnp.bfloat16


def split(value):
    high = value.astype(BF16)
    low = (value - high.astype(F32)).astype(BF16)
    return high, low


def dot(a, b):
    return jnp.dot(a, b, preferred_element_type=F32)


def product(first, high, low):
    fh, fl = split(first)
    return dot(fh, high) + (dot(fh, low) + dot(fl, high))


def kernel(
    occ_ref, off_ref, level_ref, gsteps_ref, ssteps_ref, g_ref, c_ref, h_ref,
    out_ref, w_ref,
    gbuf, occbuf, low, con, csib, part, right, left, shard, nblk, nhi, nlo, wown, wbuf,
    kf, kbuf, inv, zbuf,
    p_s, p_r, o_s, o_r, low_s, low_r, con_s, con_r, cs_s, cs_r, rr_s, rr_r, rl_s, rl_r,
    m_s, m_r, ar_s, ar_r, al_s, al_r, b_s, b_r, sib_s, sib_r, w_s, w_r, k_s, k_r, i_s, i_r,
):
    energy = lax.axis_index("energy")
    slab = lax.axis_index("slab")
    rep = lax.axis_index("rep")
    x, z = energy % XN, energy // XN
    yh, core = slab // 2, slab % 2
    zc, zb = z % 4, z // 4
    xh, xl = x // 2, x % 2

    def device(dx=0, dz=0, yh_=None, core_=None, rep_=None, x_=None):
        xx = (x + dx + XN) % XN if x_ is None else x_
        zz = (z + dz + ZN) % ZN
        yy = yh if yh_ is None else yh_
        cc = core if core_ is None else core_
        rr = rep if rep_ is None else rep_
        return (zz * XN + xx, yy * 2 + cc, rr)

    def remote(src, dst, send, recv, dev):
        return pltpu.make_async_remote_copy(
            src_ref=src, dst_ref=dst, send_sem=send, recv_sem=recv,
            device_id=dev, device_id_type=MESH,
        )

    def arrived(dst, send, recv):
        remote(dst, dst, send, recv, device(dx=1)).wait_recv()

    pending = []

    def go(*args):
        copy = remote(*args)
        copy.start()
        pending.append(copy)

    barrier = pltpu.get_barrier_semaphore()
    peers = [
        device(dx=dx, core_=(core + dc) % 2, rep_=(rep + dr) % 2)
        for dx in range(4) for dc in range(2) for dr in range(2) if (dx, dc, dr) != (0, 0, 0)
    ]
    peers += [device(dx=dx, dz=dz) for dz in (1, -1, 2, -2) for dx in range(4)]
    peers += [device(dz=4), device(dz=-4), device(yh_=1 - yh, core_=1 - core)]
    for dev in peers:
        pl.semaphore_signal(barrier, inc=1, device_id=dev, device_id_type=MESH)
    occbuf[0] = jnp.full((8, 128), occ_ref[0], F32)
    pl.semaphore_wait(barrier, len(peers))

    for slot in (0, 4, 1, 3, 2):
        dz = 2 - slot
        for dx in range(4):
            if dz == 0 and dx == 0:
                continue
            xd = (x + dx) % XN
            row = 4 * ((z + dz + ZN) % 4) + xd
            go(g_ref.at[row], gbuf.at[slot * 4 + x], p_s.at[slot, dx], p_r.at[slot, dx],
               device(dx=dx, dz=dz))
            if slot > 0:
                go(occbuf.at[0], occbuf.at[slot * 4 + x], o_s.at[slot, dx], o_r.at[slot, dx],
                   device(dx=dx, dz=dz))
    gbuf[8 + x] = g_ref[4 * zc + x]
    occbuf[8 + x] = jnp.full((8, 128), occ_ref[0], F32)
    go(g_ref, con.at[0], con_s.at[0], con_r.at[0], device(core_=1 - core))
    go(g_ref, con.at[1], con_s.at[1], con_r.at[1], device(yh_=1 - yh, core_=1 - core))
    go(c_ref.at[1 - core], csib, cs_s.at[0], cs_r.at[0], device(core_=1 - core))

    for slot in range(5):
        for dx in range(4):
            if slot == 2 and dx == 0:
                continue
            src_x = (x - dx + XN) % XN
            arrived(gbuf.at[slot * 4 + src_x], p_s.at[slot, dx], p_r.at[slot, dx])
            if slot > 0:
                arrived(occbuf.at[slot * 4 + src_x], o_s.at[slot, dx], o_r.at[slot, dx])

    offs = [jnp.clip(off_ref[f], 1, 4) for f in range(2)]

    def add_energy(n, carry):
        ee = 4 * ((z + n // 4 - 2 + ZN) % ZN) + n % 4
        cur = gbuf[n].astype(F32) * occbuf[n][0:1, 0:1]
        res = []
        for f in range(2):
            lowered = gbuf[n - offs[f]].astype(F32)
            valid = jnp.where(ee >= offs[f], 1.0, 0.0).astype(F32)
            res.append(carry[f] + cur * (lowered * valid))
        return tuple(res)

    zero = jnp.zeros((16, B), F32)
    acc = lax.fori_loop(4, 20, add_energy, (zero, zero))
    for f in range(2):
        for cb in range(4):
            part[4 * ((f + xh) % 2) + cb] = acc[f][:, 128 * cb:128 * cb + 128]

    for s in range(4):
        tr = (zb + 4 - s) % 8
        if s == 0:
            go(part.at[tr], right.at[0], rr_s.at[0], rr_r.at[0], device(dz=4))
        else:
            arrived(right.at[s - 1], rr_s.at[s - 1], rr_r.at[s - 1])
            right[s - 1] = right[s - 1] + part[tr]
            go(right.at[s - 1], right.at[s], rr_s.at[s], rr_r.at[s], device(dz=4))
        if s < 3:
            tl = (zb + 5 + s) % 8
            if s == 0:
                go(part.at[tl], left.at[0], rl_s.at[0], rl_r.at[0], device(dz=-4))
            else:
                arrived(left.at[s - 1], rl_s.at[s - 1], rl_r.at[s - 1])
                left[s - 1] = left[s - 1] + part[tl]
                go(left.at[s - 1], left.at[s], rl_s.at[s], rl_r.at[s], device(dz=-4))
        d = 4 - s
        up = energy + d
        up = jnp.where(up >= E, up - E, up)
        go(g_ref, low.at[d - 1], low_s.at[d - 1], low_r.at[d - 1], (up, slab, rep))
    arrived(left.at[2], rl_s.at[2], rl_r.at[2])
    arrived(right.at[3], rr_s.at[3], rr_r.at[3])
    total = (right[3] + left[2] + part[zb]) * (E ** -0.5)

    ft = (zb // 4 + xh) % 2
    row16 = 4 * zc + x
    c_rows = c_ref[row16 // 8, pl.ds(pl.multiple_of((row16 % 8) * 16, 16), 16),
                   pl.ds(pl.multiple_of((zb % 4) * 128, 128), 128)]
    sh, sl = split((B ** -0.5) * c_rows * total)
    shard[0] = sh
    shard[1] = sl
    xt = 2 * ft + core
    slot_n = nblk.at[rep, zc, zb, xl]
    own = jnp.logical_and(xt == x, core == rep)
    self_copy = pltpu.make_async_copy(shard, slot_n, m_r.at[xl])
    same_copy = remote(shard, slot_n, m_s.at[0], m_r.at[xl], device(x_=xt, core_=rep))
    pl.when(own)(self_copy.start)
    pl.when(jnp.logical_not(own))(same_copy.start)
    go(shard, slot_n, m_s.at[1], m_r.at[xl], device(x_=xt, core_=rep, rep_=1 - rep))
    for xs in range(2):
        arrived(nblk.at[core, zc, zb, xs], m_s.at[0], m_r.at[xs])

    dirs = (1, -1, 2)

    def to_window(block, index):
        for di, dz in enumerate(dirs):
            go(block, block, b_s.at[di, index], b_r.at[di, index], device(dz=dz))

    mine = nblk.at[core, zc, zb]
    go(mine, mine, ar_s.at[0], ar_r.at[0], device(dz=4))
    go(mine, mine, al_s.at[0], al_r.at[0], device(dz=-4))
    to_window(mine, 0)
    for s in range(4):
        block = nblk.at[core, zc, (zb + 7 - s) % 8]
        arrived(block, ar_s.at[s], ar_r.at[s])
        if s < 3:
            go(block, block, ar_s.at[s + 1], ar_r.at[s + 1], device(dz=4))
        to_window(block, 1 + s)
        if s < 3:
            block = nblk.at[core, zc, (zb + 1 + s) % 8]
            arrived(block, al_s.at[s], al_r.at[s])
            if s < 2:
                go(block, block, al_s.at[s + 1], al_r.at[s + 1], device(dz=-4))
            to_window(block, 5 + s)
    sibling = device(core_=1 - core)
    go(nblk.at[core, zc], nblk.at[core, zc], sib_s.at[0], sib_r.at[0], sibling)
    for di, dz in enumerate(dirs):
        zs = (z - dz + ZN) % ZN
        ks, js = zs // 4, zs % 4
        for index in range(8):
            kk = (ks + 8 - index if index < 5 else ks + index - 4) % 8
            arrived(nblk.at[core, js, kk], b_s.at[di, index], b_r.at[di, index])
        go(nblk.at[core, js], nblk.at[core, js], sib_s.at[1 + di], sib_r.at[1 + di], sibling)
    for n, dz in enumerate((0,) + dirs):
        js = (z - dz + ZN) % 4
        arrived(nblk.at[1 - core, js], sib_s.at[n], sib_r.at[n])

    def assemble(n, _):
        for p in range(2):
            for xs in range(2):
                for cb in range(4):
                    kk = 4 * ((xh + p) % 2) + cb
                    rows = pl.ds(pl.multiple_of(n * 64 + 32 * p + 16 * xs, 16), 16)
                    nhi[rows, 128 * cb:128 * cb + 128] = nblk[n // 4, n % 4, kk, xs, 0]
                    nlo[rows, 128 * cb:128 * cb + 128] = nblk[n // 4, n % 4, kk, xs, 1]
        return 0

    lax.fori_loop(0, 8, assemble, 0)

    arrived(csib, cs_s.at[0], cs_r.at[0])
    local = xl == core
    cw = jnp.where(local, c_ref[core], csib[...])
    count = ssteps_ref[xh]
    u1 = product(cw, nhi[...], nlo[...])
    u2 = product(u1, nhi[...], nlo[...])
    u3 = product(u2, nhi[...], nlo[...])
    w1 = cw - u1
    w2 = w1 + (u2 - u3)
    wown[...] = jnp.where(count >= 2, w2, jnp.where(count >= 1, w1, cw)).astype(BF16)
    slot_w = wbuf.at[xh, core]
    w_self = pltpu.make_async_copy(wown, slot_w, w_r.at[xh, core])
    w_sib = remote(wown, slot_w, w_s.at[0], w_r.at[xh, core], device(core_=xl))
    for dx in (1, 3, 2):
        go(wown, slot_w, w_s.at[dx], w_r.at[xh, core], device(dx=dx, core_=xl))
    pl.when(local)(w_self.start)
    pl.when(jnp.logical_not(local))(w_sib.start)

    for d in range(4):
        arrived(low.at[d], low_s.at[d], low_r.at[d])
    for n in range(2):
        arrived(con.at[n], con_s.at[n], con_r.at[n])
    for f in range(2):
        for half in range(2):
            arrived(wbuf.at[f, half], w_s.at[0], w_r.at[f, half])

    scale = B ** -0.5
    valid = [jnp.where(energy >= offs[f], scale, 0.0).astype(F32) for f in range(2)]
    inside = jnp.where(jnp.logical_or(slab == 0, slab == 3), 0.0, 0.5 * scale).astype(F32)
    level = level_ref[0]
    lane = lax.broadcasted_iota(jnp.int32, (32, B), 1)
    line = lax.broadcasted_iota(jnp.int32, (32, B), 0) + rep * H

    def operator(n, carry):
        pair = pl.ds(2 * n, 2)
        rows = pl.ds(pl.multiple_of(n * 32, 32), 32)
        half_rows = pl.ds(pl.multiple_of((n % 4) * 32, 32), 32)
        diag = lane == line + n * 32
        self_energy = jnp.zeros((32, B), F32)
        for f in range(2):
            lw = low[offs[f] - 1, pair].reshape(32, B).astype(F32)
            wf = wbuf[f, n // 4, half_rows, :].astype(F32)
            self_energy = self_energy + lw * wf * valid[f]
        contact = (con[0, pair].reshape(32, B).astype(F32) * (0.5 * scale)
                   + con[1, pair].reshape(32, B).astype(F32) * inside)
        dyson = jnp.where(diag, level, 0.0) + h_ref[rows, :] - self_energy - contact
        dd = jnp.sum(jnp.where(diag, dyson, 0.0), axis=1, keepdims=True)
        iv = 1.0 / dd
        kk = jnp.where(diag, 0.0, dyson * iv)
        kf[rows, :] = kk
        kh, kl = split(kk)
        kbuf[rep, 0, rows, :] = kh
        kbuf[rep, 1, rows, :] = kl
        return carry + jnp.sum(jnp.where(diag, iv, 0.0), axis=0, keepdims=True)

    inv_row = lax.fori_loop(0, 8, operator, jnp.zeros((1, B), F32))
    inv[0] = jnp.broadcast_to(inv_row, (8, B))
    partner = device(rep_=1 - rep)
    go(kbuf.at[rep], kbuf.at[rep], k_s.at[0], k_r.at[0], partner)
    go(inv.at[0], inv.at[1], i_s.at[0], i_r.at[0], partner)
    for f in range(2):
        for half in range(2):
            w_ref[f, 128 * half:128 * half + 128, :] = wbuf[f, half]

    def columns(r):
        return pl.ds(pl.multiple_of(r * H, H), H)

    def partial(r):
        return product(kf[:, columns(r)], kbuf[r, 0], kbuf[r, 1])

    zbuf[...] = partial(rep)
    arrived(kbuf.at[1 - rep], k_s.at[0], k_r.at[0])
    arrived(inv.at[1], i_s.at[0], i_r.at[0])
    zbuf[...] = zbuf[...] + partial(1 - rep)
    cube = (product(zbuf[:, 0:H], kbuf[0, 0], kbuf[0, 1])
            + product(zbuf[:, H:B], kbuf[1, 0], kbuf[1, 1]))
    inv_all = inv[0][0:1, :] + inv[1][0:1, :]
    twice = gsteps_ref[0] >= 2
    full_lane = lax.broadcasted_iota(jnp.int32, (H, B), 1)
    full_line = lax.broadcasted_iota(jnp.int32, (H, B), 0) + rep * H
    ident = jnp.where(full_lane == full_line, 1.0, 0.0).astype(F32)
    first = ident - kf[...]
    out_ref[...] = jnp.where(twice, first + (zbuf[...] - cube), first) * inv_all

    for copy in pending:
        copy.wait_send()
    pl.when(jnp.logical_not(own))(same_copy.wait_send)
    pl.when(jnp.logical_not(local))(w_sib.wait_send)


def body(green_blocks, occupation, offsets, coulomb, hamiltonian, onsite_level, green_steps,
         screen_steps):
    smem = pl.BlockSpec(memory_space=pltpu.SMEM)
    vmem = pl.BlockSpec(memory_space=pltpu.VMEM)
    dma = pltpu.SemaphoreType.DMA
    sems = []
    for shape in ((5, 4), (5, 4), (4,), (2,), (1,), (4,), (3,), (2,), (4,), (3,), (3, 8), (4,)):
        sems += [dma(shape), dma(shape)]
    sems += [dma((4,)), dma((2, 2)), dma((1,)), dma((1,)), dma((1,)), dma((1,))]
    green, screened = pl.pallas_call(
        kernel,
        out_shape=(
            jax.ShapeDtypeStruct((H, B), F32),
            jax.ShapeDtypeStruct((2, H, B), BF16),
        ),
        in_specs=[smem] * 5 + [vmem] * 3,
        out_specs=(vmem, vmem),
        scratch_shapes=[
            pltpu.VMEM((20, 16, B), BF16),
            pltpu.VMEM((20, 8, 128), F32),
            pltpu.VMEM((4, 16, 16, B), BF16),
            pltpu.VMEM((2, 16, 16, B), BF16),
            pltpu.VMEM((128, B), F32),
            pltpu.VMEM((8, 16, 128), F32),
            pltpu.VMEM((4, 16, 128), F32),
            pltpu.VMEM((3, 16, 128), F32),
            pltpu.VMEM((2, 16, 128), BF16),
            pltpu.VMEM((2, 4, 8, 2, 2, 16, 128), BF16),
            pltpu.VMEM((B, B), BF16),
            pltpu.VMEM((B, B), BF16),
            pltpu.VMEM((128, B), BF16),
            pltpu.VMEM((2, 2, 128, B), BF16),
            pltpu.VMEM((H, B), F32),
            pltpu.VMEM((2, 2, H, B), BF16),
            pltpu.VMEM((2, 8, B), F32),
            pltpu.VMEM((H, B), F32),
        ] + sems,
        compiler_params=pltpu.CompilerParams(
            collective_id=0, has_side_effects=True, vmem_limit_bytes=40 << 20
        ),
        name="gw_step",
    )(
        occupation, offsets, onsite_level, green_steps, screen_steps,
        green_blocks.reshape(16, 16, B), coulomb.reshape(2, 128, B), hamiltonian.reshape(H, B),
    )
    return green.reshape(1, 1, H, B), screened.reshape(2, 1, H, B)


def solution(mesh):
    return jax.shard_map(
        body,
        mesh=mesh,
        in_specs=(
            P("energy", "slab", "rep", None),
            P("energy"),
            P(),
            P("slab", "rep", None),
            P("slab", "rep", None),
            P("energy"),
            P("energy"),
            P(),
        ),
        out_specs=(P("energy", "slab", "rep", None), P(None, "slab", "rep", None)),
        check_vma=False,
    )
```

time: 1440 us -> 117 us (0.08)
  the two profiles are of different devices: /device:TPU:6 before, /device:TPU:3 now
where the time goes in v1:
time: 117 us; the launch traced here: 116 us
  Pallas kernels  108 us (92%)
  local copies, waits for them, and re-layouts  5.28 us (5%)
  between operations  2.6 us (2%)
    pallas_call x1, Pallas kernels, body(): pl.pallas_call(kernel, out_shape=(jax.ShapeDtypeStruct((H, B), F32), jax....  108 us
    unnamed x12, local copies, waits for them, and re-layouts  5.28 us

profile of v1, /device:TPU:3, one launch (start us, length us, event | category | flops | bytes accessed | tf_op | source)
XLA Modules:
  0.0 116.3 jit_solution(12179961331431006604)
XLA Ops:
  2.6 0.0 copy-start.3
  2.6 0.0 copy-start.4
  2.6 0.6 copy-done.3
  3.2 0.0 copy-done.4
  3.2 0.0 copy-start
  3.2 1.0 copy-done
  4.3 0.0 copy-start.1
  4.3 1.0 copy-done.1
  5.3 0.0 copy-start.2
  5.3 0.9 copy-done.2
  6.3 108.4 %gw_step.1 = (f32[256,512]{1,0:T(8,128)S(1)}, bf16[2,256,512]{2,1,0:T(8,128)(2,1)S(1)}) custom-call(f32[1]{0:T(128)S(6)} %copy.13.occ_ref, s32[2]{0:T(128)S(1)} %copy-done.3, f32[1]{0:T(128)S(6)} %copy.14.level_ref, s32[1]{0:T(128)S(6)} %copy.15.gsteps_ref, s32[2]{0:T(128)S(1)} %copy-done.4, bf16[16,16,512]{2,1,0:T(8,128)(2,1)S(1)} %bitcast.11, ...), custom_call_target="tpu_custom_call" | custom-call | tf_op jit(solution)/shard_map/gw_step/pallas_call | solution.py:319
  114.7 0.8 copy.16
  115.5 0.8 copy.17
Async XLA Ops:
  2.6 0.7 copy-start.3
  2.6 0.7 copy-start.4
  3.2 1.0 copy-start
  4.3 1.0 copy-start.1
  5.3 0.9 copy-start.2

commit v2 on v1

--- a/solution.py
+++ b/solution.py
@@ -32,12 +32,12 @@
 
 
 def kernel(
-    occ_ref, off_ref, level_ref, gsteps_ref, ssteps_ref, g_ref, c_ref, h_ref,
+    occ_ref, off_ref, level_ref, gsteps_ref, ssteps_ref, g_any, c_any, h_any,
     out_ref, w_ref,
-    gbuf, occbuf, low, con, csib, part, right, left, shard, nblk, nhi, nlo, wown, wbuf,
+    g_ref, c_ref, h_ref, gbuf, occbuf, low, con, csib, part, rs, shard, nblk, nhi, nlo, wown, wbuf,
     kf, kbuf, inv, zbuf,
-    p_s, p_r, o_s, o_r, low_s, low_r, con_s, con_r, cs_s, cs_r, rr_s, rr_r, rl_s, rl_r,
-    m_s, m_r, ar_s, ar_r, al_s, al_r, b_s, b_r, sib_s, sib_r, w_s, w_r, k_s, k_r, i_s, i_r,
+    p_s, p_r, o_s, o_r, low_s, low_r, con_s, con_r, cs_s, cs_r, rs_s, rs_r,
+    m_s, m_r, f_s, f_r, b_s, b_r, sib_s, sib_r, w_s, w_r, k_s, k_r, i_s, i_r, in_s, tok,
 ):
     energy = lax.axis_index("energy")
     slab = lax.axis_index("slab")
@@ -70,6 +70,11 @@
         copy = remote(*args)
         copy.start()
         pending.append(copy)
+
+    load_g = pltpu.make_async_copy(g_any, g_ref, in_s.at[0])
+    load_c = pltpu.make_async_copy(c_any, c_ref, in_s.at[1])
+    load_h = pltpu.make_async_copy(h_any, h_ref, in_s.at[2])
+    load_g.start()
 
     barrier = pltpu.get_barrier_semaphore()
     peers = [
@@ -81,7 +86,12 @@
     for dev in peers:
         pl.semaphore_signal(barrier, inc=1, device_id=dev, device_id_type=MESH)
     occbuf[0] = jnp.full((8, 128), occ_ref[0], F32)
+    load_c.start()
+    load_h.start()
+    load_g.wait()
     pl.semaphore_wait(barrier, len(peers))
+    for dz in (4, -4):
+        pl.semaphore_signal(tok, inc=1, device_id=device(dz=dz), device_id_type=MESH)
 
     for slot in (0, 4, 1, 3, 2):
         dz = 2 - slot
@@ -95,10 +105,12 @@
             if slot > 0:
                 go(occbuf.at[0], occbuf.at[slot * 4 + x], o_s.at[slot, dx], o_r.at[slot, dx],
                    device(dx=dx, dz=dz))
+    go(g_ref, low.at[3], low_s.at[3], low_r.at[3], device(dz=1))
     gbuf[8 + x] = g_ref[4 * zc + x]
     occbuf[8 + x] = jnp.full((8, 128), occ_ref[0], F32)
     go(g_ref, con.at[0], con_s.at[0], con_r.at[0], device(core_=1 - core))
     go(g_ref, con.at[1], con_s.at[1], con_r.at[1], device(yh_=1 - yh, core_=1 - core))
+    load_c.wait()
     go(c_ref.at[1 - core], csib, cs_s.at[0], cs_r.at[0], device(core_=1 - core))
 
     for slot in range(5):
@@ -128,29 +140,31 @@
         for cb in range(4):
             part[4 * ((f + xh) % 2) + cb] = acc[f][:, 128 * cb:128 * cb + 128]
 
-    for s in range(4):
-        tr = (zb + 4 - s) % 8
-        if s == 0:
-            go(part.at[tr], right.at[0], rr_s.at[0], rr_r.at[0], device(dz=4))
-        else:
-            arrived(right.at[s - 1], rr_s.at[s - 1], rr_r.at[s - 1])
-            right[s - 1] = right[s - 1] + part[tr]
-            go(right.at[s - 1], right.at[s], rr_s.at[s], rr_r.at[s], device(dz=4))
-        if s < 3:
-            tl = (zb + 5 + s) % 8
-            if s == 0:
-                go(part.at[tl], left.at[0], rl_s.at[0], rl_r.at[0], device(dz=-4))
-            else:
-                arrived(left.at[s - 1], rl_s.at[s - 1], rl_r.at[s - 1])
-                left[s - 1] = left[s - 1] + part[tl]
-                go(left.at[s - 1], left.at[s], rl_s.at[s], rl_r.at[s], device(dz=-4))
-        d = 4 - s
-        up = energy + d
-        up = jnp.where(up >= E, up - E, up)
-        go(g_ref, low.at[d - 1], low_s.at[d - 1], low_r.at[d - 1], (up, slab, rep))
-    arrived(left.at[2], rl_s.at[2], rl_r.at[2])
-    arrived(right.at[3], rr_s.at[3], rr_r.at[3])
-    total = (right[3] + left[2] + part[zb]) * (E ** -0.5)
+    def shard_of(shift):
+        return (zb + shift + 8) % 8
+
+    pl.semaphore_wait(tok, 2)
+    go(part.at[shard_of(4)], rs.at[0], rs_s.at[0], rs_r.at[0], device(dz=8))
+    go(part.at[shard_of(3)], rs.at[1], rs_s.at[1], rs_r.at[1], device(dz=8))
+    go(part.at[shard_of(-3)], rs.at[2], rs_s.at[2], rs_r.at[2], device(dz=-8))
+    go(part.at[shard_of(-2)], rs.at[3], rs_s.at[3], rs_r.at[3], device(dz=-8))
+
+    def to_row(dx, src):
+        return remote(src, low.at[dx - 1], low_s.at[dx - 1], low_r.at[dx - 1], device(dx=dx))
+
+    for dx in (1, 2, 3):
+        pl.when(x + dx < XN)(to_row(dx, g_ref).start)
+
+    for buf, shift, dst, dz in ((0, 2, 5, 8), (1, 1, 4, 4), (2, -1, 6, -4)):
+        arrived(rs.at[buf], rs_s.at[buf], rs_r.at[buf])
+        rs[buf] = rs[buf] + part[shard_of(shift)]
+        go(rs.at[buf], rs.at[dst], rs_s.at[dst], rs_r.at[dst], device(dz=dz))
+    arrived(low.at[3], low_s.at[3], low_r.at[3])
+    for dx in (1, 2, 3):
+        pl.when(x + dx >= XN)(to_row(dx, low.at[3]).start)
+    for buf in (3, 4, 6, 5):
+        arrived(rs.at[buf], rs_s.at[buf], rs_r.at[buf])
+    total = (rs[3] + rs[4] + rs[5] + rs[6] + part[zb]) * (E ** -0.5)
 
     ft = (zb // 4 + xh) % 2
     row16 = 4 * zc + x
@@ -162,13 +176,16 @@
     xt = 2 * ft + core
     slot_n = nblk.at[rep, zc, zb, xl]
     own = jnp.logical_and(xt == x, core == rep)
-    self_copy = pltpu.make_async_copy(shard, slot_n, m_r.at[xl])
-    same_copy = remote(shard, slot_n, m_s.at[0], m_r.at[xl], device(x_=xt, core_=rep))
+    self_copy = pltpu.make_async_copy(shard, slot_n, m_r.at[0, xl])
+    same_copy = remote(shard, slot_n, m_s.at[0, 0], m_r.at[0, xl], device(x_=xt, core_=rep))
+    shifts = (0, 1, -1, 2, -2)
+    for m in (3, 4, 1, 2):
+        for other in range(2):
+            go(shard, slot_n, m_s.at[m, other], m_r.at[m, xl],
+               device(dz=4 * shifts[m], x_=xt, core_=rep, rep_=(rep + other) % 2))
     pl.when(own)(self_copy.start)
     pl.when(jnp.logical_not(own))(same_copy.start)
-    go(shard, slot_n, m_s.at[1], m_r.at[xl], device(x_=xt, core_=rep, rep_=1 - rep))
-    for xs in range(2):
-        arrived(nblk.at[core, zc, zb, xs], m_s.at[0], m_r.at[xs])
+    go(shard, slot_n, m_s.at[0, 1], m_r.at[0, xl], device(x_=xt, core_=rep, rep_=1 - rep))
 
     dirs = (1, -1, 2)
 
@@ -176,29 +193,31 @@
         for di, dz in enumerate(dirs):
             go(block, block, b_s.at[di, index], b_r.at[di, index], device(dz=dz))
 
-    mine = nblk.at[core, zc, zb]
-    go(mine, mine, ar_s.at[0], ar_r.at[0], device(dz=4))
-    go(mine, mine, al_s.at[0], al_r.at[0], device(dz=-4))
-    to_window(mine, 0)
-    for s in range(4):
-        block = nblk.at[core, zc, (zb + 7 - s) % 8]
-        arrived(block, ar_s.at[s], ar_r.at[s])
-        if s < 3:
-            go(block, block, ar_s.at[s + 1], ar_r.at[s + 1], device(dz=4))
-        to_window(block, 1 + s)
-        if s < 3:
-            block = nblk.at[core, zc, (zb + 1 + s) % 8]
-            arrived(block, al_s.at[s], al_r.at[s])
-            if s < 2:
-                go(block, block, al_s.at[s + 1], al_r.at[s + 1], device(dz=-4))
-            to_window(block, 5 + s)
+    def own_block(shift):
+        return nblk.at[core, zc, shard_of(-shift)]
+
+    for m in range(5):
+        block = own_block(shifts[m])
+        for xs in range(2):
+            arrived(nblk.at[core, zc, shard_of(-shifts[m]), xs], m_s.at[m, 0], m_r.at[m, xs])
+        if shifts[m] == 2:
+            go(block, block, f_s.at[1], f_r.at[1], device(dz=8))
+            go(block, block, f_s.at[0], f_r.at[0], device(dz=4))
+        if shifts[m] == -2:
+            go(block, block, f_s.at[2], f_r.at[2], device(dz=-4))
+        to_window(block, m)
+    far = (3, -3, 4)
+    for n, (shift, sem) in enumerate(((3, 0), (-3, 2), (4, 1))):
+        block = own_block(shift)
+        arrived(block, f_s.at[sem], f_r.at[sem])
+        to_window(block, 5 + n)
     sibling = device(core_=1 - core)
     go(nblk.at[core, zc], nblk.at[core, zc], sib_s.at[0], sib_r.at[0], sibling)
     for di, dz in enumerate(dirs):
         zs = (z - dz + ZN) % ZN
         ks, js = zs // 4, zs % 4
-        for index in range(8):
-            kk = (ks + 8 - index if index < 5 else ks + index - 4) % 8
+        for index, shift in enumerate(shifts + far):
+            kk = (ks - shift + 8) % 8
             arrived(nblk.at[core, js, kk], b_s.at[di, index], b_r.at[di, index])
         go(nblk.at[core, js], nblk.at[core, js], sib_s.at[1 + di], sib_r.at[1 + di], sibling)
     for n, dz in enumerate((0,) + dirs):
@@ -235,7 +254,7 @@
     pl.when(local)(w_self.start)
     pl.when(jnp.logical_not(local))(w_sib.start)
 
-    for d in range(4):
+    for d in range(3):
         arrived(low.at[d], low_s.at[d], low_r.at[d])
     for n in range(2):
         arrived(con.at[n], con_s.at[n], con_r.at[n])
@@ -243,6 +262,7 @@
         for half in range(2):
             arrived(wbuf.at[f, half], w_s.at[0], w_r.at[f, half])
 
+    load_h.wait()
     scale = B ** -0.5
     valid = [jnp.where(energy >= offs[f], scale, 0.0).astype(F32) for f in range(2)]
     inside = jnp.where(jnp.logical_or(slab == 0, slab == 3), 0.0, 0.5 * scale).astype(F32)
@@ -303,6 +323,8 @@
 
     for copy in pending:
         copy.wait_send()
+    for dx in (1, 2, 3):
+        to_row(dx, g_ref).wait_send()
     pl.when(jnp.logical_not(own))(same_copy.wait_send)
     pl.when(jnp.logical_not(local))(w_sib.wait_send)
 
@@ -310,29 +332,33 @@
 def body(green_blocks, occupation, offsets, coulomb, hamiltonian, onsite_level, green_steps,
          screen_steps):
     smem = pl.BlockSpec(memory_space=pltpu.SMEM)
+    hbm = pl.BlockSpec(memory_space=pl.ANY)
     vmem = pl.BlockSpec(memory_space=pltpu.VMEM)
     dma = pltpu.SemaphoreType.DMA
     sems = []
-    for shape in ((5, 4), (5, 4), (4,), (2,), (1,), (4,), (3,), (2,), (4,), (3,), (3, 8), (4,)):
+    for shape in ((5, 4), (5, 4), (4,), (2,), (1,), (7,), (5, 2), (3,), (3, 8), (4,)):
         sems += [dma(shape), dma(shape)]
-    sems += [dma((4,)), dma((2, 2)), dma((1,)), dma((1,)), dma((1,)), dma((1,))]
+    sems += [dma((4,)), dma((2, 2)), dma((1,)), dma((1,)), dma((1,)), dma((1,)), dma((3,)),
+             pltpu.SemaphoreType.REGULAR]
     green, screened = pl.pallas_call(
         kernel,
         out_shape=(
             jax.ShapeDtypeStruct((H, B), F32),
             jax.ShapeDtypeStruct((2, H, B), BF16),
         ),
-        in_specs=[smem] * 5 + [vmem] * 3,
+        in_specs=[smem] * 5 + [hbm] * 3,
         out_specs=(vmem, vmem),
         scratch_shapes=[
+            pltpu.VMEM((16, 16, B), BF16),
+            pltpu.VMEM((2, 128, B), F32),
+            pltpu.VMEM((H, B), F32),
             pltpu.VMEM((20, 16, B), BF16),
             pltpu.VMEM((20, 8, 128), F32),
             pltpu.VMEM((4, 16, 16, B), BF16),
             pltpu.VMEM((2, 16, 16, B), BF16),
             pltpu.VMEM((128, B), F32),
             pltpu.VMEM((8, 16, 128), F32),
-            pltpu.VMEM((4, 16, 128), F32),
-            pltpu.VMEM((3, 16, 128), F32),
+            pltpu.VMEM((7, 16, 128), F32),
             pltpu.VMEM((2, 16, 128), BF16),
             pltpu.VMEM((2, 4, 8, 2, 2, 16, 128), BF16),
             pltpu.VMEM((B, B), BF16),
@@ -345,7 +371,7 @@
             pltpu.VMEM((H, B), F32),
         ] + sems,
         compiler_params=pltpu.CompilerParams(
-            collective_id=0, has_side_effects=True, vmem_limit_bytes=40 << 20
+            collective_id=0, has_side_effects=True, vmem_limit_bytes=62 << 20
         ),
         name="gw_step",
     )(

time: 117 us -> 102 us (0.87)
  the two profiles are of different devices: /device:TPU:3 before, /device:TPU:6 now
where the time goes in v2:
time: 102 us
  Pallas kernels  96.6 us (95%)
  local copies, waits for them, and re-layouts  2.72 us (3%)
  between operations  2.58 us (3%)
    pallas_call x1, Pallas kernels, body(): pl.pallas_call(kernel, out_shape=(jax.ShapeDtypeStruct((H, B), F32), jax....  96.6 us
    unnamed x4, local copies, waits for them, and re-layouts  2.72 us

profile of v2, /device:TPU:6, one launch (start us, length us, event | category | flops | bytes accessed | tf_op | source)
XLA Modules:
  0.0 101.9 jit_solution(13354160267835279732)
XLA Ops:
  2.6 96.6 %gw_step.1 = (f32[256,512]{1,0:T(8,128)}, bf16[2,256,512]{2,1,0:T(8,128)(2,1)}) custom-call(f32[1]{0:T(128)S(6)} %copy.13.occ_ref, s32[2]{0:T(128)} %off_ref.1, f32[1]{0:T(128)S(6)} %copy.14.level_ref, s32[1]{0:T(128)S(6)} %copy.15.gsteps_ref, s32[2]{0:T(128)} %ssteps_ref.1, bf16[16,16,512]{2,1,0:T(8,128)(2,1)} %bitcast.11, f32[2,128,512]{2,1,0:T(8,128)} %bitcast.7, ...), custom_call_target="tpu_custom_call" | custom-call | tf_op jit(solution)/shard_map/gw_step/pallas_call | solution.py:343
  99.2 0.0 copy-start
  99.2 1.9 %copy.16 = f32[1,1,256,512]{3,2,1,0:T(8,128)} copy(f32[1,1,256,512]{3,2,1,0:T(8,128)} %bitcast.10) | data formatting | bytes 1048576
  101.1 0.0 copy-done
  101.1 0.8 copy.17
Async XLA Ops:
  99.2 1.9 %copy-start = (bf16[2,256,512]{2,1,0:T(8,128)(2,1)S(1)}, bf16[2,256,512]{2,1,0:T(8,128)(2,1)}, u32[]{:S(2)}) copy-start(bf16[2,256,512]{2,1,0:T(8,128)(2,1)} %get-tuple-element.5) | copy-start | bytes 1572868

commit v3 on v2

--- a/solution.py
+++ b/solution.py
@@ -34,10 +34,10 @@
 def kernel(
     occ_ref, off_ref, level_ref, gsteps_ref, ssteps_ref, g_any, c_any, h_any,
     out_ref, w_ref,
-    g_ref, c_ref, h_ref, gbuf, occbuf, low, con, csib, part, rs, shard, nblk, nhi, nlo, wown, wbuf,
-    kf, kbuf, inv, zbuf,
+    g_ref, c_ref, h_ref, gbuf, occbuf, low, con, cbuf, part, rs, shard, nblk, nhi, nlo, wown, wbuf,
+    kf, kbuf, base, lsel, zbuf,
     p_s, p_r, o_s, o_r, low_s, low_r, con_s, con_r, cs_s, cs_r, rs_s, rs_r,
-    m_s, m_r, f_s, f_r, b_s, b_r, sib_s, sib_r, w_s, w_r, k_s, k_r, i_s, i_r, in_s, tok,
+    m_s, m_r, f_s, f_r, b_s, b_r, sib_s, sib_r, w_s, w_r, e_s, e_r, in_s, tok,
 ):
     energy = lax.axis_index("energy")
     slab = lax.axis_index("slab")
@@ -111,7 +111,15 @@
     go(g_ref, con.at[0], con_s.at[0], con_r.at[0], device(core_=1 - core))
     go(g_ref, con.at[1], con_s.at[1], con_r.at[1], device(yh_=1 - yh, core_=1 - core))
     load_c.wait()
-    go(c_ref.at[1 - core], csib, cs_s.at[0], cs_r.at[0], device(core_=1 - core))
+    holds = core == xl
+    c_self = pltpu.make_async_copy(c_ref, cbuf, cs_r.at[0])
+    c_same = remote(c_ref, cbuf, cs_s.at[0], cs_r.at[0], device(core_=rep))
+    c_other = remote(c_ref, cbuf, cs_s.at[1], cs_r.at[0], device(core_=rep, rep_=1 - rep))
+    c_here = jnp.logical_and(holds, core == rep)
+    c_there = jnp.logical_and(holds, core != rep)
+    pl.when(c_here)(c_self.start)
+    pl.when(c_there)(c_same.start)
+    pl.when(holds)(c_other.start)
 
     for slot in range(5):
         for dx in range(4):
@@ -154,6 +162,28 @@
 
     for dx in (1, 2, 3):
         pl.when(x + dx < XN)(to_row(dx, g_ref).start)
+
+    for n in range(2):
+        arrived(con.at[n], con_s.at[n], con_r.at[n])
+    load_h.wait()
+    scale = B ** -0.5
+    inside = jnp.where(jnp.logical_or(slab == 0, slab == 3), 0.0, 0.5 * scale).astype(F32)
+    level = level_ref[0]
+    lane = lax.broadcasted_iota(jnp.int32, (32, B), 1)
+    line = lax.broadcasted_iota(jnp.int32, (32, B), 0)
+    partner = device(rep_=1 - rep)
+
+    def base_rows(n, _):
+        pair = pl.ds(2 * n, 2)
+        rows = pl.ds(pl.multiple_of(n * 32, 32), 32)
+        contact = (con[0, pair].reshape(32, B).astype(F32) * (0.5 * scale)
+                   + con[1, pair].reshape(32, B).astype(F32) * inside)
+        diag = lane == line + (rep * H + n * 32)
+        base[rep, rows, :] = jnp.where(diag, level, 0.0) + h_ref[rows, :] - contact
+        return 0
+
+    lax.fori_loop(0, 8, base_rows, 0)
+    go(base.at[rep], base.at[rep], e_s.at[0], e_r.at[0], partner)
 
     for buf, shift, dst, dz in ((0, 2, 5, 8), (1, 1, 4, 4), (2, -1, 6, -4)):
         arrived(rs.at[buf], rs_s.at[buf], rs_r.at[buf])
@@ -211,8 +241,20 @@
         block = own_block(shift)
         arrived(block, f_s.at[sem], f_r.at[sem])
         to_window(block, 5 + n)
+    for d in range(3):
+        arrived(low.at[d], low_s.at[d], low_r.at[d])
+
+    def pick_rows(n, _):
+        rows = pl.ds(pl.multiple_of(n * 32, 32), 32)
+        for f in range(2):
+            lw = low[offs[f] - 1, pl.ds(2 * n, 2)].reshape(32, B).astype(F32)
+            lsel[rep, f, rows, :] = jnp.where(energy >= offs[f], lw, 0.0).astype(BF16)
+        return 0
+
     sibling = device(core_=1 - core)
     go(nblk.at[core, zc], nblk.at[core, zc], sib_s.at[0], sib_r.at[0], sibling)
+    lax.fori_loop(0, 8, pick_rows, 0)
+    go(lsel.at[rep], lsel.at[rep], e_s.at[1], e_r.at[1], partner)
     for di, dz in enumerate(dirs):
         zs = (z - dz + ZN) % ZN
         ks, js = zs // 4, zs % 4
@@ -236,9 +278,9 @@
 
     lax.fori_loop(0, 8, assemble, 0)
 
-    arrived(csib, cs_s.at[0], cs_r.at[0])
+    arrived(cbuf, cs_s.at[0], cs_r.at[0])
     local = xl == core
-    cw = jnp.where(local, c_ref[core], csib[...])
+    cw = cbuf[...].reshape(H, B)
     count = ssteps_ref[xh]
     u1 = product(cw, nhi[...], nlo[...])
     u2 = product(u1, nhi[...], nlo[...])
@@ -254,71 +296,41 @@
     pl.when(local)(w_self.start)
     pl.when(jnp.logical_not(local))(w_sib.start)
 
-    for d in range(3):
-        arrived(low.at[d], low_s.at[d], low_r.at[d])
-    for n in range(2):
-        arrived(con.at[n], con_s.at[n], con_r.at[n])
+    for n, buf in enumerate((base, lsel)):
+        arrived(buf.at[1 - rep], e_s.at[n], e_r.at[n])
     for f in range(2):
         for half in range(2):
             arrived(wbuf.at[f, half], w_s.at[0], w_r.at[f, half])
 
-    load_h.wait()
-    scale = B ** -0.5
-    valid = [jnp.where(energy >= offs[f], scale, 0.0).astype(F32) for f in range(2)]
-    inside = jnp.where(jnp.logical_or(slab == 0, slab == 3), 0.0, 0.5 * scale).astype(F32)
-    level = level_ref[0]
-    lane = lax.broadcasted_iota(jnp.int32, (32, B), 1)
-    line = lax.broadcasted_iota(jnp.int32, (32, B), 0) + rep * H
-
     def operator(n, carry):
-        pair = pl.ds(2 * n, 2)
-        rows = pl.ds(pl.multiple_of(n * 32, 32), 32)
-        half_rows = pl.ds(pl.multiple_of((n % 4) * 32, 32), 32)
+        r = n // 8
+        rows = pl.ds(pl.multiple_of((n % 8) * 32, 32), 32)
+        self_energy = (lsel[r, 0, rows, :].astype(F32) * wbuf[0, r, rows, :].astype(F32)
+                       + lsel[r, 1, rows, :].astype(F32) * wbuf[1, r, rows, :].astype(F32)) * scale
+        dyson = base[r, rows, :] - self_energy
         diag = lane == line + n * 32
-        self_energy = jnp.zeros((32, B), F32)
-        for f in range(2):
-            lw = low[offs[f] - 1, pair].reshape(32, B).astype(F32)
-            wf = wbuf[f, n // 4, half_rows, :].astype(F32)
-            self_energy = self_energy + lw * wf * valid[f]
-        contact = (con[0, pair].reshape(32, B).astype(F32) * (0.5 * scale)
-                   + con[1, pair].reshape(32, B).astype(F32) * inside)
-        dyson = jnp.where(diag, level, 0.0) + h_ref[rows, :] - self_energy - contact
         dd = jnp.sum(jnp.where(diag, dyson, 0.0), axis=1, keepdims=True)
         iv = 1.0 / dd
         kk = jnp.where(diag, 0.0, dyson * iv)
-        kf[rows, :] = kk
+        kf[r, rows, :] = kk
         kh, kl = split(kk)
-        kbuf[rep, 0, rows, :] = kh
-        kbuf[rep, 1, rows, :] = kl
+        kbuf[r, 0, rows, :] = kh
+        kbuf[r, 1, rows, :] = kl
         return carry + jnp.sum(jnp.where(diag, iv, 0.0), axis=0, keepdims=True)
 
-    inv_row = lax.fori_loop(0, 8, operator, jnp.zeros((1, B), F32))
-    inv[0] = jnp.broadcast_to(inv_row, (8, B))
-    partner = device(rep_=1 - rep)
-    go(kbuf.at[rep], kbuf.at[rep], k_s.at[0], k_r.at[0], partner)
-    go(inv.at[0], inv.at[1], i_s.at[0], i_r.at[0], partner)
+    inv_all = lax.fori_loop(0, 16, operator, jnp.zeros((1, B), F32))
     for f in range(2):
-        for half in range(2):
-            w_ref[f, 128 * half:128 * half + 128, :] = wbuf[f, half]
-
-    def columns(r):
-        return pl.ds(pl.multiple_of(r * H, H), H)
-
-    def partial(r):
-        return product(kf[:, columns(r)], kbuf[r, 0], kbuf[r, 1])
-
-    zbuf[...] = partial(rep)
-    arrived(kbuf.at[1 - rep], k_s.at[0], k_r.at[0])
-    arrived(inv.at[1], i_s.at[0], i_r.at[0])
-    zbuf[...] = zbuf[...] + partial(1 - rep)
+        w_ref[f] = wbuf[f, rep]
+
+    zbuf[...] = (product(kf[rep, :, 0:H], kbuf[0, 0], kbuf[0, 1])
+                 + product(kf[rep, :, H:B], kbuf[1, 0], kbuf[1, 1]))
     cube = (product(zbuf[:, 0:H], kbuf[0, 0], kbuf[0, 1])
             + product(zbuf[:, H:B], kbuf[1, 0], kbuf[1, 1]))
-    inv_all = inv[0][0:1, :] + inv[1][0:1, :]
     twice = gsteps_ref[0] >= 2
     full_lane = lax.broadcasted_iota(jnp.int32, (H, B), 1)
     full_line = lax.broadcasted_iota(jnp.int32, (H, B), 0) + rep * H
     ident = jnp.where(full_lane == full_line, 1.0, 0.0).astype(F32)
-    first = ident - kf[...]
+    first = ident - kf[rep]
     out_ref[...] = jnp.where(twice, first + (zbuf[...] - cube), first) * inv_all
 
     for copy in pending:
@@ -327,6 +339,8 @@
         to_row(dx, g_ref).wait_send()
     pl.when(jnp.logical_not(own))(same_copy.wait_send)
     pl.when(jnp.logical_not(local))(w_sib.wait_send)
+    pl.when(c_there)(c_same.wait_send)
+    pl.when(holds)(c_other.wait_send)
 
 
 def body(green_blocks, occupation, offsets, coulomb, hamiltonian, onsite_level, green_steps,
@@ -336,9 +350,9 @@
     vmem = pl.BlockSpec(memory_space=pltpu.VMEM)
     dma = pltpu.SemaphoreType.DMA
     sems = []
-    for shape in ((5, 4), (5, 4), (4,), (2,), (1,), (7,), (5, 2), (3,), (3, 8), (4,)):
+    for shape in ((5, 4), (5, 4), (4,), (2,), (2,), (7,), (5, 2), (3,), (3, 8), (4,)):
         sems += [dma(shape), dma(shape)]
-    sems += [dma((4,)), dma((2, 2)), dma((1,)), dma((1,)), dma((1,)), dma((1,)), dma((3,)),
+    sems += [dma((4,)), dma((2, 2)), dma((2,)), dma((2,)), dma((3,)),
              pltpu.SemaphoreType.REGULAR]
     green, screened = pl.pallas_call(
         kernel,
@@ -356,18 +370,19 @@
             pltpu.VMEM((20, 8, 128), F32),
             pltpu.VMEM((4, 16, 16, B), BF16),
             pltpu.VMEM((2, 16, 16, B), BF16),
-            pltpu.VMEM((128, B), F32),
+            pltpu.VMEM((2, 128, B), F32),
             pltpu.VMEM((8, 16, 128), F32),
             pltpu.VMEM((7, 16, 128), F32),
             pltpu.VMEM((2, 16, 128), BF16),
             pltpu.VMEM((2, 4, 8, 2, 2, 16, 128), BF16),
             pltpu.VMEM((B, B), BF16),
             pltpu.VMEM((B, B), BF16),
-            pltpu.VMEM((128, B), BF16),
-            pltpu.VMEM((2, 2, 128, B), BF16),
-            pltpu.VMEM((H, B), F32),
+            pltpu.VMEM((H, B), BF16),
             pltpu.VMEM((2, 2, H, B), BF16),
-            pltpu.VMEM((2, 8, B), F32),
+            pltpu.VMEM((2, H, B), F32),
+            pltpu.VMEM((2, 2, H, B), BF16),
+            pltpu.VMEM((2, H, B), F32),
+            pltpu.VMEM((2, 2, H, B), BF16),
             pltpu.VMEM((H, B), F32),
         ] + sems,
         compiler_params=pltpu.CompilerParams(

time: 102 us -> 99.5 us (0.975)
  the two profiles are of different devices: /device:TPU:6 before, /device:TPU:16 now
where the time goes in v3:
time: 99.5 us; the launch traced here: 99.2 us
  Pallas kernels  93.9 us (94%)
  local copies, waits for them, and re-layouts  2.72 us (3%)
  between operations  2.58 us (3%)
    pallas_call x1, Pallas kernels, body(): pl.pallas_call(kernel, out_shape=(jax.ShapeDtypeStruct((H, B), F32), jax....  93.9 us
    unnamed x4, local copies, waits for them, and re-layouts  2.72 us

profile of v3, /device:TPU:16, one launch (start us, length us, event | category | flops | bytes accessed | tf_op | source)
XLA Modules:
  0.0 99.2 jit_solution(2954986774339787636)
XLA Ops:
  2.6 93.9 %gw_step.1 = (f32[256,512]{1,0:T(8,128)}, bf16[2,256,512]{2,1,0:T(8,128)(2,1)}) custom-call(f32[1]{0:T(128)S(6)} %copy.13.occ_ref, s32[2]{0:T(128)} %off_ref.1, f32[1]{0:T(128)S(6)} %copy.14.level_ref, s32[1]{0:T(128)S(6)} %copy.15.gsteps_ref, s32[2]{0:T(128)} %ssteps_ref.1, bf16[16,16,512]{2,1,0:T(8,128)(2,1)} %bitcast.11, f32[2,128,512]{2,1,0:T(8,128)} %bitcast.7, ...), custom_call_target="tpu_custom_call" | custom-call | tf_op jit(solution)/shard_map/gw_step/pallas_call | solution.py:357
  96.5 0.0 copy-start
  96.5 1.9 %copy.16 = f32[1,1,256,512]{3,2,1,0:T(8,128)} copy(f32[1,1,256,512]{3,2,1,0:T(8,128)} %bitcast.10) | data formatting | bytes 1048576
  98.5 0.0 copy-done
  98.5 0.8 copy.17
Async XLA Ops:
  96.5 1.9 %copy-start = (bf16[2,256,512]{2,1,0:T(8,128)(2,1)S(1)}, bf16[2,256,512]{2,1,0:T(8,128)(2,1)}, u32[]{:S(2)}) copy-start(bf16[2,256,512]{2,1,0:T(8,128)(2,1)} %get-tuple-element.5) | copy-start | bytes 1572868

commit v4 on v3

--- a/solution.py
+++ b/solution.py
@@ -203,7 +203,12 @@
     sh, sl = split((B ** -0.5) * c_rows * total)
     shard[0] = sh
     shard[1] = sl
-    xt = 2 * ft + core
+    fm = (xh + rep) % 2
+
+    def column(rep_):
+        return 2 * ((ft + rep_) % 2) + core
+
+    xt = column(rep)
     slot_n = nblk.at[rep, zc, zb, xl]
     own = jnp.logical_and(xt == x, core == rep)
     self_copy = pltpu.make_async_copy(shard, slot_n, m_r.at[0, xl])
@@ -212,10 +217,12 @@
     for m in (3, 4, 1, 2):
         for other in range(2):
             go(shard, slot_n, m_s.at[m, other], m_r.at[m, xl],
-               device(dz=4 * shifts[m], x_=xt, core_=rep, rep_=(rep + other) % 2))
+               device(dz=4 * shifts[m], x_=column((rep + other) % 2), core_=rep,
+                      rep_=(rep + other) % 2))
     pl.when(own)(self_copy.start)
     pl.when(jnp.logical_not(own))(same_copy.start)
-    go(shard, slot_n, m_s.at[0, 1], m_r.at[0, xl], device(x_=xt, core_=rep, rep_=1 - rep))
+    go(shard, slot_n, m_s.at[0, 1], m_r.at[0, xl],
+       device(x_=column(1 - rep), core_=rep, rep_=1 - rep))
 
     dirs = (1, -1, 2)
 
@@ -236,11 +243,6 @@
         if shifts[m] == -2:
             go(block, block, f_s.at[2], f_r.at[2], device(dz=-4))
         to_window(block, m)
-    far = (3, -3, 4)
-    for n, (shift, sem) in enumerate(((3, 0), (-3, 2), (4, 1))):
-        block = own_block(shift)
-        arrived(block, f_s.at[sem], f_r.at[sem])
-        to_window(block, 5 + n)
     for d in range(3):
         arrived(low.at[d], low_s.at[d], low_r.at[d])
 
@@ -251,10 +253,15 @@
             lsel[rep, f, rows, :] = jnp.where(energy >= offs[f], lw, 0.0).astype(BF16)
         return 0
 
+    lax.fori_loop(0, 8, pick_rows, 0)
+    go(lsel.at[rep], lsel.at[rep], e_s.at[1], e_r.at[1], partner)
+    far = (3, -3, 4)
+    for n, (shift, sem) in enumerate(((3, 0), (-3, 2), (4, 1))):
+        block = own_block(shift)
+        arrived(block, f_s.at[sem], f_r.at[sem])
+        to_window(block, 5 + n)
     sibling = device(core_=1 - core)
     go(nblk.at[core, zc], nblk.at[core, zc], sib_s.at[0], sib_r.at[0], sibling)
-    lax.fori_loop(0, 8, pick_rows, 0)
-    go(lsel.at[rep], lsel.at[rep], e_s.at[1], e_r.at[1], partner)
     for di, dz in enumerate(dirs):
         zs = (z - dz + ZN) % ZN
         ks, js = zs // 4, zs % 4
@@ -270,7 +277,7 @@
         for p in range(2):
             for xs in range(2):
                 for cb in range(4):
-                    kk = 4 * ((xh + p) % 2) + cb
+                    kk = 4 * ((fm + p) % 2) + cb
                     rows = pl.ds(pl.multiple_of(n * 64 + 32 * p + 16 * xs, 16), 16)
                     nhi[rows, 128 * cb:128 * cb + 128] = nblk[n // 4, n % 4, kk, xs, 0]
                     nlo[rows, 128 * cb:128 * cb + 128] = nblk[n // 4, n % 4, kk, xs, 1]
@@ -281,18 +288,19 @@
     arrived(cbuf, cs_s.at[0], cs_r.at[0])
     local = xl == core
     cw = cbuf[...].reshape(H, B)
-    count = ssteps_ref[xh]
+    count = ssteps_ref[fm]
     u1 = product(cw, nhi[...], nlo[...])
     u2 = product(u1, nhi[...], nlo[...])
     u3 = product(u2, nhi[...], nlo[...])
     w1 = cw - u1
     w2 = w1 + (u2 - u3)
     wown[...] = jnp.where(count >= 2, w2, jnp.where(count >= 1, w1, cw)).astype(BF16)
-    slot_w = wbuf.at[xh, core]
-    w_self = pltpu.make_async_copy(wown, slot_w, w_r.at[xh, core])
-    w_sib = remote(wown, slot_w, w_s.at[0], w_r.at[xh, core], device(core_=xl))
-    for dx in (1, 3, 2):
-        go(wown, slot_w, w_s.at[dx], w_r.at[xh, core], device(dx=dx, core_=xl))
+    slot_w = wbuf.at[fm, core]
+    w_self = pltpu.make_async_copy(wown, slot_w, w_r.at[fm, core])
+    w_sib = remote(wown, slot_w, w_s.at[0], w_r.at[fm, core], device(core_=xl))
+    for n, dev in enumerate((device(dx=1, core_=xl), device(dx=-1, core_=xl),
+                             device(core_=xl, rep_=1 - rep))):
+        go(wown, slot_w, w_s.at[1 + n], w_r.at[fm, core], dev)
     pl.when(local)(w_self.start)
     pl.when(jnp.logical_not(local))(w_sib.start)
 

time: 99.5 us -> 92.2 us (0.927)
  the two profiles are of different devices: /device:TPU:16 before, /device:TPU:6 now
where the time goes in v4:
time: 92.2 us; the launch traced here: 91.4 us
  Pallas kernels  86.1 us (93%)
  local copies, waits for them, and re-layouts  2.72 us (3%)
  between operations  2.58 us (3%)
    pallas_call x1, Pallas kernels, body(): pl.pallas_call(kernel, out_shape=(jax.ShapeDtypeStruct((H, B), F32), jax....  86.1 us
    unnamed x4, local copies, waits for them, and re-layouts  2.72 us

profile of v4, /device:TPU:6, one launch (start us, length us, event | category | flops | bytes accessed | tf_op | source)
XLA Modules:
  0.0 91.4 jit_solution(17934655033857741519)
XLA Ops:
  2.6 86.1 %gw_step.1 = (f32[256,512]{1,0:T(8,128)}, bf16[2,256,512]{2,1,0:T(8,128)(2,1)}) custom-call(f32[1]{0:T(128)S(6)} %copy.13.occ_ref, s32[2]{0:T(128)} %off_ref.1, f32[1]{0:T(128)S(6)} %copy.14.level_ref, s32[1]{0:T(128)S(6)} %copy.15.gsteps_ref, s32[2]{0:T(128)} %ssteps_ref.1, bf16[16,16,512]{2,1,0:T(8,128)(2,1)} %bitcast.11, f32[2,128,512]{2,1,0:T(8,128)} %bitcast.7, ...), custom_call_target="tpu_custom_call" | custom-call | tf_op jit(solution)/shard_map/gw_step/pallas_call | solution.py:365
  88.6 0.0 copy-start
  88.6 1.9 %copy.16 = f32[1,1,256,512]{3,2,1,0:T(8,128)} copy(f32[1,1,256,512]{3,2,1,0:T(8,128)} %bitcast.10) | data formatting | bytes 1048576
  90.6 0.0 copy-done
  90.6 0.8 copy.17
Async XLA Ops:
  88.6 1.9 %copy-start = (bf16[2,256,512]{2,1,0:T(8,128)(2,1)S(1)}, bf16[2,256,512]{2,1,0:T(8,128)(2,1)}, u32[]{:S(2)}) copy-start(bf16[2,256,512]{2,1,0:T(8,128)(2,1)} %get-tuple-element.5) | copy-start | bytes 1572868

commit v5 on v4

--- a/solution.py
+++ b/solution.py
@@ -33,7 +33,7 @@
 
 def kernel(
     occ_ref, off_ref, level_ref, gsteps_ref, ssteps_ref, g_any, c_any, h_any,
-    out_ref, w_ref,
+    out_ref, w_ref, inv_ref,
     g_ref, c_ref, h_ref, gbuf, occbuf, low, con, cbuf, part, rs, shard, nblk, nhi, nlo, wown, wbuf,
     kf, kbuf, base, lsel, zbuf,
     p_s, p_r, o_s, o_r, low_s, low_r, con_s, con_r, cs_s, cs_r, rs_s, rs_r,
@@ -105,11 +105,18 @@
             if slot > 0:
                 go(occbuf.at[0], occbuf.at[slot * 4 + x], o_s.at[slot, dx], o_r.at[slot, dx],
                    device(dx=dx, dz=dz))
-    go(g_ref, low.at[3], low_s.at[3], low_r.at[3], device(dz=1))
     gbuf[8 + x] = g_ref[4 * zc + x]
     occbuf[8 + x] = jnp.full((8, 128), occ_ref[0], F32)
     go(g_ref, con.at[0], con_s.at[0], con_r.at[0], device(core_=1 - core))
-    go(g_ref, con.at[1], con_s.at[1], con_r.at[1], device(yh_=1 - yh, core_=1 - core))
+    edge = jnp.logical_or(slab == 0, slab == 3)
+    beside = remote(g_ref, con.at[1], con_s.at[1], con_r.at[1],
+                    device(yh_=1 - yh, core_=1 - core))
+    pl.when(jnp.logical_not(edge))(beside.start)
+
+    @pl.when(edge)
+    def _():
+        con[1] = jnp.zeros((16, 16, B), BF16)
+
     load_c.wait()
     holds = core == xl
     c_self = pltpu.make_async_copy(c_ref, cbuf, cs_r.at[0])
@@ -156,6 +163,7 @@
     go(part.at[shard_of(3)], rs.at[1], rs_s.at[1], rs_r.at[1], device(dz=8))
     go(part.at[shard_of(-3)], rs.at[2], rs_s.at[2], rs_r.at[2], device(dz=-8))
     go(part.at[shard_of(-2)], rs.at[3], rs_s.at[3], rs_r.at[3], device(dz=-8))
+    go(g_ref, low.at[3], low_s.at[3], low_r.at[3], device(dz=1))
 
     def to_row(dx, src):
         return remote(src, low.at[dx - 1], low_s.at[dx - 1], low_r.at[dx - 1], device(dx=dx))
@@ -163,8 +171,15 @@
     for dx in (1, 2, 3):
         pl.when(x + dx < XN)(to_row(dx, g_ref).start)
 
-    for n in range(2):
-        arrived(con.at[n], con_s.at[n], con_r.at[n])
+    for buf, shift, dst, dz in ((0, 2, 5, 8), (1, 1, 4, 4), (2, -1, 6, -4)):
+        arrived(rs.at[buf], rs_s.at[buf], rs_r.at[buf])
+        rs[buf] = rs[buf] + part[shard_of(shift)]
+        go(rs.at[buf], rs.at[dst], rs_s.at[dst], rs_r.at[dst], device(dz=dz))
+    arrived(low.at[3], low_s.at[3], low_r.at[3])
+    for dx in (1, 2, 3):
+        pl.when(x + dx >= XN)(to_row(dx, low.at[3]).start)
+    arrived(con.at[0], con_s.at[0], con_r.at[0])
+    pl.when(jnp.logical_not(edge))(beside.wait_recv)
     load_h.wait()
     scale = B ** -0.5
     inside = jnp.where(jnp.logical_or(slab == 0, slab == 3), 0.0, 0.5 * scale).astype(F32)
@@ -185,13 +200,6 @@
     lax.fori_loop(0, 8, base_rows, 0)
     go(base.at[rep], base.at[rep], e_s.at[0], e_r.at[0], partner)
 
-    for buf, shift, dst, dz in ((0, 2, 5, 8), (1, 1, 4, 4), (2, -1, 6, -4)):
-        arrived(rs.at[buf], rs_s.at[buf], rs_r.at[buf])
-        rs[buf] = rs[buf] + part[shard_of(shift)]
-        go(rs.at[buf], rs.at[dst], rs_s.at[dst], rs_r.at[dst], device(dz=dz))
-    arrived(low.at[3], low_s.at[3], low_r.at[3])
-    for dx in (1, 2, 3):
-        pl.when(x + dx >= XN)(to_row(dx, low.at[3]).start)
     for buf in (3, 4, 6, 5):
         arrived(rs.at[buf], rs_s.at[buf], rs_r.at[buf])
     total = (rs[3] + rs[4] + rs[5] + rs[6] + part[zb]) * (E ** -0.5)
@@ -339,7 +347,8 @@
     full_line = lax.broadcasted_iota(jnp.int32, (H, B), 0) + rep * H
     ident = jnp.where(full_lane == full_line, 1.0, 0.0).astype(F32)
     first = ident - kf[rep]
-    out_ref[...] = jnp.where(twice, first + (zbuf[...] - cube), first) * inv_all
+    out_ref[...] = jnp.where(twice, first + (zbuf[...] - cube), first)
+    inv_ref[...] = jnp.broadcast_to(inv_all, (8, B))
 
     for copy in pending:
         copy.wait_send()
@@ -348,6 +357,7 @@
     pl.when(jnp.logical_not(own))(same_copy.wait_send)
     pl.when(jnp.logical_not(local))(w_sib.wait_send)
     pl.when(c_there)(c_same.wait_send)
+    pl.when(jnp.logical_not(edge))(beside.wait_send)
     pl.when(holds)(c_other.wait_send)
 
 
@@ -362,14 +372,15 @@
         sems += [dma(shape), dma(shape)]
     sems += [dma((4,)), dma((2, 2)), dma((2,)), dma((2,)), dma((3,)),
              pltpu.SemaphoreType.REGULAR]
-    green, screened = pl.pallas_call(
+    green, screened, scales = pl.pallas_call(
         kernel,
         out_shape=(
             jax.ShapeDtypeStruct((H, B), F32),
             jax.ShapeDtypeStruct((2, H, B), BF16),
+            jax.ShapeDtypeStruct((8, B), F32),
         ),
         in_specs=[smem] * 5 + [hbm] * 3,
-        out_specs=(vmem, vmem),
+        out_specs=(vmem, vmem, vmem),
         scratch_shapes=[
             pltpu.VMEM((16, 16, B), BF16),
             pltpu.VMEM((2, 128, B), F32),
@@ -401,6 +412,7 @@
         occupation, offsets, onsite_level, green_steps, screen_steps,
         green_blocks.reshape(16, 16, B), coulomb.reshape(2, 128, B), hamiltonian.reshape(H, B),
     )
+    green = green * scales[0:1]
     return green.reshape(1, 1, H, B), screened.reshape(2, 1, H, B)
 
 

time: 92.2 us -> 93.1 us (level)
  other arithmetic: 0 us -> 1.96 us
  local copies, waits for them, and re-layouts: 2.72 us -> 1.52 us
    reshape x0 -> x1, other arithmetic: none -> 1.96 us  [body(): return (green.reshape(1, 1, H, B), screened.reshape(2, 1, H, B))]
    unnamed x4 -> x3, local copies, waits for them, and re-layouts: 2.72 us -> 0.8 us
where the time goes in v5:
time: 93.1 us; the launch traced here: 92 us
  Pallas kernels  85.9 us (92%)
  between operations  2.58 us (3%)
  other arithmetic  1.96 us (2%)
  local copies, waits for them, and re-layouts  1.52 us (2%)
    pallas_call x1, Pallas kernels, body(): pl.pallas_call(kernel, out_shape=(jax.ShapeDtypeStruct((H, B), F32), jax....  85.9 us
    reshape x1, other arithmetic, body(): return (green.reshape(1, 1, H, B), screened.reshape(2, 1, H, B))  1.96 us

profile of v5, /device:TPU:6, one launch (start us, length us, event | category | flops | bytes accessed | tf_op | source)
XLA Modules:
  0.0 92.0 jit_solution(4368108506792036657)
XLA Ops:
  2.6 85.9 %gw_step.1 = (f32[256,512]{1,0:T(8,128)}, bf16[2,256,512]{2,1,0:T(8,128)(2,1)}, f32[8,512]{1,0:T(8,128)}) custom-call(f32[1]{0:T(128)S(6)} %copy.12.occ_ref, s32[2]{0:T(128)} %off_ref.1, f32[1]{0:T(128)S(6)} %copy.13.level_ref, s32[1]{0:T(128)S(6)} %copy.14.gsteps_ref, s32[2]{0:T(128)} %ssteps_ref.1, bf16[16,16,512]{2,1,0:T(8,128)(2,1)} %bitcast.12, ...), custom_call_target="tpu_custom_call" | custom-call | tf_op jit(solution)/shard_map/gw_step/pallas_call | solution.py:375
  88.5 0.7 slice.3
  89.2 0.0 copy-start
  89.2 2.0 %multiply_bitcast_fusion = f32[1,1,256,512]{3,2,1,0:T(8,128)} fusion(f32[256,512]{1,0:T(8,128)} %get-tuple-element.5, f32[512]{0:T(512)S(1)} %bitcast.13), kind=kLoop, calls=%fused_computation | loop fusion | flops 131072 | bytes 1050624 | tf_op jit(solution)/shard_map/reshape | solution.py:416
  91.2 0.0 copy-done
  91.2 0.8 copy.15
Async XLA Ops:
  89.2 2.0 %copy-start = (bf16[2,256,512]{2,1,0:T(8,128)(2,1)S(1)}, bf16[2,256,512]{2,1,0:T(8,128)(2,1)}, u32[]{:S(2)}) copy-start(bf16[2,256,512]{2,1,0:T(8,128)(2,1)} %get-tuple-element.7) | copy-start | bytes 1572868
